TPU v7x, 32 devices: a whole 2x2x4 slice. The times are simulated.
32 devices in a mesh: row: 16 (over z, x, core), col: 2 (over y).
Axes of the slice: x: 2, y: 2, z: 4, core: 2. Of those that a mesh axis runs over, the one named last changes fastest.
Arguments:
- alignment_activations: bfloat16 [64, 768, 256], P(None, ('row', 'col')), may hold values from -60 to 60
- layer_norm_gain: float32 [256], replicated, may hold values from 0.5 to 1.5
- layer_norm_bias: float32 [256], replicated, may hold values from -3 to 3
- left_weight: bfloat16 [256, 32], replicated, may hold values from -0.375 to 0.375
- left_operand_bias: float32 [32], replicated, may hold values from -3 to 3
- right_weight: bfloat16 [256, 32], replicated, may hold values from -0.375 to 0.375
- right_operand_bias: float32 [32], replicated, may hold values from -3 to 3
- output_weight: bfloat16 [1024, 128], replicated, may hold values from -0.75 to 0.75
- output_bias_vector: float32 [128], replicated, may hold values from -3 to 3
- pair_cotangent: bfloat16 [768, 768, 128], P('row', 'col'), may hold values from -6 to 6
Outputs:
- pair_output_update: bfloat16 [768, 768, 128], P('row', 'col')
- alignment_gradient: bfloat16 [64, 768, 256], P(None, ('row', 'col'))
- output_weight_gradient: float32 [1024, 128], replicated
All inputs are finite; a program needn't handle non-finite values.
Results may differ from a plain program's by a relative error of at most 0.028.
Values may be sent and summed in bfloat16 or wider, within the bound.
A program may use at most 64 MiB of HBM per device.

v0:
```python
import jax
import jax.numpy as jnp
from jax import lax
from jax.sharding import PartitionSpec as P

IBLK = 8


def apply_layer_norm(alignment_activations, layer_norm_gain, layer_norm_bias):
    input_values = alignment_activations.astype(jnp.float32)
    average = jnp.mean(input_values, axis=-1, keepdims=True)
    shifted = input_values - average
    variance = jnp.mean(shifted * shifted, axis=-1, keepdims=True)
    inverse_deviation = lax.rsqrt(variance + 1e-05)
    standardized_input = shifted * inverse_deviation
    normalized_input = (standardized_input * layer_norm_gain + layer_norm_bias).astype(jnp.bfloat16)
    return (standardized_input, inverse_deviation, normalized_input)


def project(normalized_input, weight, bias_vec):
    sequence_count, residue_count, alignment_width = normalized_input.shape
    flattened_row_matrix = normalized_input.reshape(-1, alignment_width)
    result = jnp.dot(flattened_row_matrix, weight, preferred_element_type=jnp.float32) + bias_vec
    return result.astype(jnp.bfloat16).reshape(sequence_count, residue_count, weight.shape[1])


def local(
    alignment_activations,
    layer_norm_gain,
    layer_norm_bias,
    left_weight,
    left_operand_bias,
    right_weight,
    right_operand_bias,
    output_weight,
    output_bias_vector,
    pair_cotangent,
):
    sequence_count, local_residue_block, alignment_width = alignment_activations.shape
    hidden = left_weight.shape[1]
    out_width = output_weight.shape[1]
    row_ratio = lax.axis_size("row") // lax.axis_size("col")
    row_index = lax.axis_index("row")
    col_index = lax.axis_index("col")
    standardized_input, inverse_deviation, normalized_input = apply_layer_norm(
        alignment_activations, layer_norm_gain, layer_norm_bias
    )
    left_proj = project(normalized_input, left_weight, left_operand_bias)
    right_proj = project(normalized_input, right_weight, right_operand_bias)
    left_rows, right_rows = (
        lax.all_gather(left_proj, "col", axis=1, tiled=True),
        lax.all_gather(right_proj, "col", axis=1, tiled=True),
    )
    block_len = left_rows.shape[1]
    col_span = block_len * row_ratio
    right_all = lax.all_gather(right_rows, "row", axis=1, tiled=True)
    right_cols = lax.dynamic_slice_in_dim(right_all, col_index * col_span, col_span, 1)
    factor = 1.0 / sequence_count
    blocks = block_len // IBLK
    row_blocks = left_rows.reshape(sequence_count, blocks, IBLK, hidden).transpose(1, 0, 2, 3)
    grad_blocks = pair_cotangent.reshape(blocks, IBLK, col_span, out_width)

    def block_step(carry, pieces_now):
        right_acc, weight_acc = carry
        row_block, grad_block = pieces_now
        outer_sum = jnp.einsum(
            "sip,sjq->ijpq", row_block, right_cols, preferred_element_type=jnp.float32
        )
        outer_mean = (outer_sum * factor).astype(jnp.bfloat16)
        flat_outer = outer_mean.reshape(-1, hidden * hidden)
        update = (
            jnp.dot(flat_outer, output_weight, preferred_element_type=jnp.float32)
            + output_bias_vector
        )
        update = update.astype(jnp.bfloat16).reshape(IBLK, col_span, out_width)
        flat_grad = grad_block.reshape(-1, out_width)
        weight_acc = weight_acc + jnp.einsum(
            "ak,ah->kh", flat_outer, flat_grad, preferred_element_type=jnp.float32
        )
        outer_grad = jnp.dot(flat_grad, output_weight.T, preferred_element_type=jnp.float32)
        outer_grad = outer_grad.astype(jnp.bfloat16).reshape(IBLK, col_span, hidden, hidden)
        left_block = (
            jnp.einsum("ijpq,sjq->sip", outer_grad, right_cols, preferred_element_type=jnp.float32)
            * factor
        )
        right_acc = (
            right_acc
            + jnp.einsum("ijpq,sip->sjq", outer_grad, row_block, preferred_element_type=jnp.float32)
            * factor
        )
        return ((right_acc, weight_acc), (update, left_block))

    initial = (
        jnp.zeros((sequence_count, col_span, hidden), jnp.float32),
        jnp.zeros((hidden * hidden, out_width), jnp.float32),
    )
    (right_part, weight_part), (updates, left_blocks) = lax.scan(
        block_step, initial, (row_blocks, grad_blocks)
    )
    pair_output_update = updates.reshape(block_len, col_span, out_width)
    left_part = left_blocks.transpose(1, 0, 2, 3).reshape(sequence_count, block_len, hidden)
    col_total = lax.psum(right_part.astype(jnp.bfloat16), "row").astype(jnp.float32)
    right_sum = lax.dynamic_slice_in_dim(col_total, row_index % row_ratio * block_len, block_len, 1)
    owner = (row_index // row_ratio == col_index).astype(jnp.float32)
    right_sum = right_sum * owner
    left_grad, right_grad = (
        lax.psum_scatter(
            left_part.astype(jnp.bfloat16), "col", scatter_dimension=1, tiled=True
        ).astype(jnp.float32),
        lax.psum_scatter(
            right_sum.astype(jnp.bfloat16), "col", scatter_dimension=1, tiled=True
        ).astype(jnp.float32),
    )
    output_weight_gradient = lax.psum(weight_part, ("row", "col"))
    normalized_gradient = jnp.dot(
        left_grad.astype(jnp.bfloat16).reshape(-1, hidden),
        left_weight.T,
        preferred_element_type=jnp.float32,
    )
    normalized_gradient = normalized_gradient + jnp.dot(
        right_grad.astype(jnp.bfloat16).reshape(-1, hidden),
        right_weight.T,
        preferred_element_type=jnp.float32,
    )
    normalized_gradient = normalized_gradient.reshape(
        sequence_count, local_residue_block, alignment_width
    )
    scaled_gradient = normalized_gradient * layer_norm_gain
    centering_term = jnp.mean(scaled_gradient, axis=-1, keepdims=True)
    gradient_slope_term = jnp.mean(scaled_gradient * standardized_input, axis=-1, keepdims=True)
    alignment_gradient = (
        inverse_deviation
        * (scaled_gradient - centering_term - standardized_input * gradient_slope_term)
    ).astype(jnp.bfloat16)
    return (pair_output_update, alignment_gradient, output_weight_gradient)


def solution(mesh):
    in_specs = (
        P(None, ("row", "col"), None),
        P(),
        P(),
        P(),
        P(),
        P(),
        P(),
        P(),
        P(),
        P("row", "col", None),
    )
    out_specs = (P("row", "col", None), P(None, ("row", "col"), None), P())
    return jax.shard_map(local, mesh=mesh, in_specs=in_specs, out_specs=out_specs, check_vma=False)
```

profile of v0, /device:TPU:0, one launch (start us, length us, event | category | flops | bytes accessed | tf_op | source)
XLA Modules:
  0.0 594.2 jit_solution(6830450470452875657)
XLA Ops:
  12.6 8.6 %all_gather.10 = bf16[64,48,32]{0,2,1:T(8,128)(2,1)} all-gather(bf16[64,24,32]{0,2,1:T(8,128)(2,1)S(1)} %copy.46), channel_id=1, replica_groups=mesh['row'=16,'col'=2] {'col'}, dimensions={1}, use_global_device_ids=true | all-gather | bytes 294912 | tf_op jit(solution)/shard_map/all_gather | solution.py:52
  22.9 6.8 %all_gather.9 = bf16[64,48,32]{0,2,1:T(8,128)(2,1)S(1)} all-gather(bf16[64,24,32]{0,2,1:T(8,128)(2,1)S(1)} %copy.45), channel_id=1, replica_groups=mesh['row'=16,'col'=2] {'col'}, dimensions={1}, use_global_device_ids=true | all-gather | bytes 294912 | tf_op jit(solution)/shard_map/all_gather | solution.py:51
  29.6 55.1 %all-gather.2.cloned.1.call-done = bf16[64,768,32]{0,2,1:T(8,128)(2,1)} async-done(((bf16[64,48,32]{0,2,1:T(8,128)(2,1)}), bf16[64,768,32]{0,2,1:T(8,128)(2,1)}) %all-gather.2.cloned.1.call-update) | async-done | bytes 3145744 | tf_op jit(solution)/shard_map/all_gather | solution.py:56
  84.7 4.1 constant_dynamic-slice_fusion.1
  88.9 4.6 copy.47
  93.5 229.4 %while.17 = (s32[]{:T(128)}, f32[64,384,32]{1,0,2:T(8,128)}, f32[1024,128]{1,0:T(8,128)S(1)}, bf16[6,8,384,128]{3,2,1,0:T(8,128)(2,1)}, bf16[6,64,8,32]{1,3,2,0:...) while((s32[]{:T(128)}, f32[64,384,32]{1,0,2:T(8,128)}, ...), condition=%wide.region_3.4_spmd.clone, body=%wide.region_2.3_spmd.clone.sunk | while | flops 3636756480 | bytes 130024152 | solution.py:97
  106.8 4.4 convolution_convert_fusion.2
  111.3 8.7 %copy.81 = bf16[3072,1024]{0,1:T(8,128)(2,1)} copy(bf16[3072,1024]{1,0:T(8,128)(2,1)} %convolution_convert_fusion.2) | data formatting | bytes 12582912 | tf_op jit(solution)/shard_map/while/body/eval_jaxpr/convert_element_type | solution.py:81
  119.9 4.4 copy.82
  145.0 4.5 convolution_convert_fusion.2
  149.5 8.7 %copy.81 = bf16[3072,1024]{0,1:T(8,128)(2,1)} copy(bf16[3072,1024]{1,0:T(8,128)(2,1)} %convolution_convert_fusion.2) | data formatting | bytes 12582912 | tf_op jit(solution)/shard_map/while/body/eval_jaxpr/convert_element_type | solution.py:81
  158.1 4.4 copy.82
  164.4 4.0 fusion.85
  183.2 4.4 convolution_convert_fusion.2
  187.7 8.7 %copy.81 = bf16[3072,1024]{0,1:T(8,128)(2,1)} copy(bf16[3072,1024]{1,0:T(8,128)(2,1)} %convolution_convert_fusion.2) | data formatting | bytes 12582912 | tf_op jit(solution)/shard_map/while/body/eval_jaxpr/convert_element_type | solution.py:81
  196.3 4.4 copy.82
  202.6 4.0 fusion.85
  221.4 4.4 convolution_convert_fusion.2
  225.9 8.7 %copy.81 = bf16[3072,1024]{0,1:T(8,128)(2,1)} copy(bf16[3072,1024]{1,0:T(8,128)(2,1)} %convolution_convert_fusion.2) | data formatting | bytes 12582912 | tf_op jit(solution)/shard_map/while/body/eval_jaxpr/convert_element_type | solution.py:81
  234.5 4.4 copy.82
  259.6 4.4 convolution_convert_fusion.2
  264.0 8.7 %copy.81 = bf16[3072,1024]{0,1:T(8,128)(2,1)} copy(bf16[3072,1024]{1,0:T(8,128)(2,1)} %convolution_convert_fusion.2) | data formatting | bytes 12582912 | tf_op jit(solution)/shard_map/while/body/eval_jaxpr/convert_element_type | solution.py:81
  272.7 4.4 copy.82
  279.0 4.0 fusion.85
  297.8 4.4 convolution_convert_fusion.2
  302.3 8.7 %copy.81 = bf16[3072,1024]{0,1:T(8,128)(2,1)} copy(bf16[3072,1024]{1,0:T(8,128)(2,1)} %convolution_convert_fusion.2) | data formatting | bytes 12582912 | tf_op jit(solution)/shard_map/while/body/eval_jaxpr/convert_element_type | solution.py:81
  310.9 4.4 copy.82
  322.9 5.0 copy.70
  328.7 93.3 %all-reduce.3.cloned.1.call-done = bf16[64,384,32]{1,2,0:T(8,128)(2,1)} async-done(((bf16[64,384,32]{1,2,0:T(8,128)(2,1)}), bf16[64,384,32]{1,2,0:T(8,128)(2,1)}) %all-reduce.3.cloned.1.call-update) | async-done | bytes 1572880 | tf_op jit(solution)/shard_map/psum | solution.py:102
  425.8 11.1 %reduce-scatter.3.cloned.1.call-done = bf16[64,24,32]{0,2,1:T(8,128)(2,1)} async-done(((bf16[64,48,32]{0,2,1:T(8,128)(2,1)}), bf16[64,24,32]{0,2,1:T(8,128)(2,1)}) %reduce-scatter.3.cloned.1.call-update) | async-done | bytes 98320 | tf_op jit(solution)/shard_map/reduce_scatter | solution.py:107
  440.5 11.8 %reduce-scatter.5.cloned.1.call-done = bf16[64,24,32]{0,2,1:T(8,128)(2,1)} async-done(((bf16[64,48,32]{0,2,1:T(8,128)(2,1)}), bf16[64,24,32]{0,2,1:T(8,128)(2,1)}) %reduce-scatter.5.cloned.1.call-update) | async-done | bytes 98320 | tf_op jit(solution)/shard_map/reduce_scatter | solution.py:110
  458.8 127.0 %all-reduce.5.cloned.1.call-done = f32[1024,128]{1,0:T(8,128)} async-done(((f32[1024,128]{1,0:T(8,128)}), f32[1024,128]{1,0:T(8,128)}) %all-reduce.5.cloned.1.call-update) | async-done | bytes 524304 | tf_op jit(solution)/shard_map/psum | solution.py:114
  (148 shorter events, 134.7 us)
Async XLA Ops:
  7.2 3.9 copy-start
  7.2 3.3 copy-start.4
  7.2 3.3 copy-start.13
  7.2 3.3 copy-start.15
  7.2 3.9 copy-start.16
  7.2 77.5 %all-gather.2.cloned.1.call-start = ((), (), s32[]{:S(2)}) async-start(), calls=%async_computation.2 | async-start | bytes 6684672 | tf_op jit(solution)/shard_map/all_gather | solution.py:56
  8.8 2.2 copy-start.7
  11.1 10.3 %copy-start.11 = (bf16[256,32]{0,1:T(8,128)(2,1)S(1)}, bf16[256,32]{0,1:T(8,128)(2,1)}, u32[]{:S(2)}) copy-start(bf16[256,32]{0,1:T(8,128)(2,1)} %param.15) | copy-start | bytes 49156
  11.1 10.3 %copy-start.17 = (f32[32]{0:T(128)S(1)}, f32[32]{0:T(128)}, u32[]{:S(2)}) copy-start(f32[32]{0:T(128)} %param.16) | copy-start | bytes 388
  21.2 400.8 %all-reduce.3.cloned.1.call-start = ((), (), s32[]{:S(2)}) async-start(), calls=%async_computation.4 | async-start | bytes 3145728 | tf_op jit(solution)/shard_map/psum | solution.py:102
  88.9 4.6 copy-start.6
  88.9 4.6 copy-start.18
  124.3 1.9 copy-start.1
  130.3 1.7 copy-start.2
  162.5 1.9 copy-start.1
  168.5 1.7 copy-start.2
  200.7 1.9 copy-start.1
  206.7 1.7 copy-start.2
  238.9 1.9 copy-start.1
  277.1 1.9 copy-start.1
  283.1 1.7 copy-start.2
  315.3 1.9 copy-start.1
  321.3 1.7 copy-start.2
  322.9 5.0 copy-start.3
  327.9 109.0 %reduce-scatter.3.cloned.1.call-start = ((), (), s32[]{:S(2)}) async-start(), calls=%async_computation.3 | async-start | bytes 589824 | tf_op jit(solution)/shard_map/reduce_scatter | solution.py:107
  328.7 123.6 %reduce-scatter.5.cloned.1.call-start = ((), (), s32[]{:S(2)}) async-start(), calls=%async_computation.5 | async-start | bytes 589824 | tf_op jit(solution)/shard_map/reduce_scatter | solution.py:110
  423.5 15.4 %copy-start.12 = (bf16[256,32]{0,1:T(8,128)(2,1)S(1)}, bf16[256,32]{0,1:T(8,128)(2,1)}, u32[]{:S(2)}) copy-start(bf16[256,32]{0,1:T(8,128)(2,1)} %param.15) | copy-start | bytes 49156
  425.2 160.6 %all-reduce.5.cloned.1.call-start = ((), (), s32[]{:S(2)}) async-start(), calls=%async_computation.6 | async-start | bytes 1048576 | tf_op jit(solution)/shard_map/psum | solution.py:114
  438.9 15.3 %copy-start.14 = (f32[256]{0:T(256)S(1)}, f32[256]{0:T(256)}, u32[]{:S(2)}) copy-start(f32[256]{0:T(256)} %param.13) | copy-start | bytes 3076
  454.2 2.1 copy-start.5
  454.2 2.1 copy-start.8
  454.3 2.1 copy-start.10
  (2 other events, 2.3 us)
Sparse Core Ops, SparseCore 0:
  21.4 63.3 all-gather.1
  328.0 93.9 all-reduce.2
  424.9 12.0 reduce-scatter.2
  439.1 13.1 reduce-scatter.4
  458.0 127.8 all-reduce.4
where the time goes:
time: 597 us; the launch traced here: 594 us
  waiting for transfers between devices  300 us (50%)
  local copies, waits for them, and re-layouts  158 us (26%)
  matrix products  98.8 us (17%)
  blocking collectives  15.4 us (3%)
  between operations  14.2 us (2%)
  other arithmetic  7.52 us (1%)
    psum x1, waiting for transfers between devices, local(): output_weight_gradient = lax.psum(weight_part, ('row', 'col'))  127 us
    psum x1, waiting for transfers between devices, local(): lax.psum(right_part.astype(jnp.bfloat16), 'row').astype(jnp.float32)  93.3 us
    all_gather x1, waiting for transfers between devices, local(): right_all = lax.all_gather(right_rows, 'row', axis=1, tiled=True)  55.1 us
    convert_element_type x6, local copies, waits for them, and re-layouts, block_step(): outer_grad.astype(jnp.bfloat16).reshape(IBLK, col_span, hidden, hidden)  51.9 us
    while x36, local copies, waits for them, and re-layouts  42.6 us
    dot_general x6, matrix products, block_step(): jnp.dot(flat_grad, output_weight.T, preferred_element_type=jnp.float32)  26.7 us
    dot_general x6, matrix products, block_step(): jnp.einsum('ijpq,sip->sjq', outer_grad, row_block, preferred_element_type...  24.2 us
    convert_element_type x6, local copies, waits for them, and re-layouts, block_step(): outer_mean = (outer_sum * factor).astype(jnp.bfloat16)  22.7 us
  transfers between devices with their start and end apart: 5, of which 5 were waited for; matrix products, arithmetic and copies ran while one was open for 2% of the time, Pallas kernels for 0%

commit v1 on v0

v1 whole, which is shorter than its diff:
```python
import functools

import jax
import jax.numpy as jnp
from jax import lax
from jax.experimental import pallas as pl
from jax.experimental.pallas import tpu as pltpu
from jax.sharding import PartitionSpec as P

BF = jnp.bfloat16
F32 = jnp.float32


def divisor_up_to(total, most):
    best = 1
    for d in range(1, most + 1):
        if total % d == 0:
            best = d
    return best


def nn(a, b):
    return lax.dot_general(a, b, (((1,), (0,)), ((), ())), preferred_element_type=F32)


def nt(a, b):
    return lax.dot_general(a, b, (((1,), (1,)), ((), ())), preferred_element_type=F32)


def mix_kernel(ib, seqs, hidden, l_ref, w_ref, dp_ref, m_ref, dr_ref, acc, wide):
    step = pl.program_id(0)
    out = dp_ref.shape[2]
    rows = l_ref[...]
    for q in range(0, hidden, 2):
        res = nn(rows, w_ref[:, q * out : (q + 2) * out]).astype(BF)
        for e in range(2):
            for i in range(ib):
                m_ref[(q + e) * seqs : (q + e + 1) * seqs, i * out : (i + 1) * out] = res[
                    i * seqs : (i + 1) * seqs, e * out : (e + 1) * out
                ]
    for i in range(ib):
        wide[:, i * out : (i + 1) * out] = dp_ref[i]

    @pl.when(step == 0)
    def _():
        acc[...] = jnp.zeros_like(acc)

    width = 256
    for c in range(0, hidden * seqs, width):
        acc[:, c : c + width] += nt(wide[...], m_ref[c : c + width, :])

    @pl.when(step == pl.num_programs(0) - 1)
    def _():
        dr_ref[...] = acc[...].astype(BF)


def grad_kernel(ib, seqs, hidden, rt_ref, dp_ref, wt_ref, lt_ref, dl_ref, dw_ref, nl, wide):
    step = pl.program_id(0)
    out = dp_ref.shape[2]
    for i in range(ib):
        wide[:, i * out : (i + 1) * out] = dp_ref[i]
    qs = 4
    for q in range(0, hidden, qs):
        res = nn(rt_ref[q * seqs : (q + qs) * seqs, :], wide[...]).astype(BF)
        for e in range(qs):
            for i in range(ib):
                nl[i * seqs : (i + 1) * seqs, (q + e) * out : (q + e + 1) * out] = res[
                    e * seqs : (e + 1) * seqs, i * out : (i + 1) * out
                ]
    dl_ref[...] = nn(nl[...], wt_ref[...]).astype(BF)

    @pl.when(step == 0)
    def _():
        dw_ref[...] = jnp.zeros_like(dw_ref)

    width = 512
    for c in range(0, hidden * out, width):
        dw_ref[:, c : c + width] += nn(lt_ref[...], nl[:, c : c + width])


def update_kernel(ib, r_ref, m_ref, b_ref, o_ref):
    out = o_ref.shape[2]
    for i in range(0, ib, 2):
        res = nn(r_ref[...], m_ref[:, i * out : (i + 2) * out])
        for e in range(2):
            o_ref[i + e] = (res[:, e * out : (e + 1) * out] + b_ref[...]).astype(BF)


def apply_layer_norm(x, gain, bias):
    v = x.astype(F32)
    average = jnp.mean(v, axis=-1, keepdims=True)
    shifted = v - average
    variance = jnp.mean(shifted * shifted, axis=-1, keepdims=True)
    inv = lax.rsqrt(variance + 1e-05)
    standard = shifted * inv
    return standard, inv, (standard * gain + bias).astype(BF)


def local(x, gain, bias, wl, bl, wr, br, wo, bo, dp):
    seqs, own, width = x.shape
    hidden = wl.shape[1]
    out = wo.shape[1]
    nrow, ncol = lax.axis_size("row"), lax.axis_size("col")
    rows, cols, _ = dp.shape
    qs = hidden * seqs
    qh = hidden * out
    factor = 1.0 / seqs

    standard, inv, normed = apply_layer_norm(x, gain, bias)
    both = nn(normed.reshape(-1, width), jnp.concatenate([wl, wr], axis=1))
    left = (both[:, :hidden] + bl).astype(BF).reshape(seqs, own, hidden)
    right = (both[:, hidden:] + br).astype(BF).reshape(seqs, own, hidden)

    left_rows = lax.all_gather(left.transpose(1, 0, 2), "col", axis=0, tiled=True)
    left_rows = left_rows.reshape(rows * seqs, hidden)

    there = [(g, (g % nrow) * ncol + g // nrow) for g in range(nrow * ncol)]
    back = [(d, g) for g, d in there]
    mine = lax.ppermute(right.transpose(1, 2, 0).reshape(own, qs), ("row", "col"), there)
    right_cols = lax.all_gather(mine, "row", axis=0, tiled=True)
    right_t = (right_cols * BF(factor)).T

    w2 = wo.reshape(hidden, qh)
    ib = divisor_up_to(rows, 4)
    steps = rows // ib
    params = pltpu.CompilerParams(vmem_limit_bytes=56 * 1024 * 1024)

    m, dr = pl.pallas_call(
        functools.partial(mix_kernel, ib, seqs, hidden),
        grid=(steps,),
        in_specs=[
            pl.BlockSpec((ib * seqs, hidden), lambda t: (t, 0)),
            pl.BlockSpec((hidden, qh), lambda t: (0, 0)),
            pl.BlockSpec((ib, cols, out), lambda t: (t, 0, 0)),
        ],
        out_specs=[
            pl.BlockSpec((qs, ib * out), lambda t: (0, t)),
            pl.BlockSpec((cols, qs), lambda t: (0, 0)),
        ],
        out_shape=[
            jax.ShapeDtypeStruct((qs, rows * out), BF),
            jax.ShapeDtypeStruct((cols, qs), BF),
        ],
        scratch_shapes=[pltpu.VMEM((cols, qs), F32), pltpu.VMEM((cols, ib * out), BF)],
        compiler_params=params,
        cost_estimate=pl.CostEstimate(flops=2 * cols * qs * rows * out, bytes_accessed=30000000, transcendentals=0),
        name="mix",
    )(left_rows, w2 * BF(factor), dp)

    dr_mine = lax.psum_scatter(dr, "row", scatter_dimension=0, tiled=True)
    dr_own = lax.ppermute(dr_mine, ("row", "col"), back)

    dl, dw = pl.pallas_call(
        functools.partial(grad_kernel, ib, seqs, hidden),
        grid=(steps,),
        in_specs=[
            pl.BlockSpec((qs, cols), lambda t: (0, 0)),
            pl.BlockSpec((ib, cols, out), lambda t: (t, 0, 0)),
            pl.BlockSpec((qh, hidden), lambda t: (0, 0)),
            pl.BlockSpec((hidden, ib * seqs), lambda t: (0, t)),
        ],
        out_specs=[
            pl.BlockSpec((ib * seqs, hidden), lambda t: (t, 0)),
            pl.BlockSpec((hidden, qh), lambda t: (0, 0)),
        ],
        out_shape=[
            jax.ShapeDtypeStruct((rows * seqs, hidden), BF),
            jax.ShapeDtypeStruct((hidden, qh), F32),
        ],
        scratch_shapes=[pltpu.VMEM((ib * seqs, qh), BF), pltpu.VMEM((cols, ib * out), BF)],
        compiler_params=params,
        cost_estimate=pl.CostEstimate(flops=2 * cols * qs * rows * out, bytes_accessed=10000000, transcendentals=0),
        name="grad",
    )(right_t, dp, w2.T, left_rows.T)

    dl_own = lax.psum_scatter(
        dl.reshape(rows, seqs * hidden), "col", scatter_dimension=0, tiled=True
    )
    dw_all = lax.psum(dw, ("row", "col"))

    update = pl.pallas_call(
        functools.partial(update_kernel, ib),
        grid=(steps,),
        in_specs=[
            pl.BlockSpec((cols, qs), lambda t: (0, 0)),
            pl.BlockSpec((qs, ib * out), lambda t: (0, t)),
            pl.BlockSpec((1, out), lambda t: (0, 0)),
        ],
        out_specs=pl.BlockSpec((ib, cols, out), lambda t: (t, 0, 0)),
        out_shape=jax.ShapeDtypeStruct((rows, cols, out), BF),
        compiler_params=params,
        cost_estimate=pl.CostEstimate(flops=2 * cols * qs * rows * out, bytes_accessed=30000000, transcendentals=0),
        name="update",
    )(right_cols, m, bo.reshape(1, out))

    dl3 = dl_own.reshape(own, seqs, hidden).transpose(1, 0, 2).reshape(-1, hidden)
    dr3 = dr_own.reshape(own, hidden, seqs).transpose(2, 0, 1).reshape(-1, hidden)
    g = nt(jnp.concatenate([dl3, dr3], axis=1), jnp.concatenate([wl, wr], axis=1))
    g = g.reshape(seqs, own, width) * gain
    centre = jnp.mean(g, axis=-1, keepdims=True)
    slope = jnp.mean(g * standard, axis=-1, keepdims=True)
    dx = (inv * (g - centre - standard * slope)).astype(BF)
    return update, dx, dw_all.reshape(hidden * hidden, out)


def solution(mesh):
    both = ("row", "col")
    in_specs = (P(None, both, None),) + (P(),) * 8 + (P("row", "col", None),)
    out_specs = (P("row", "col", None), P(None, both, None), P())
    return jax.shard_map(local, mesh=mesh, in_specs=in_specs, out_specs=out_specs, check_vma=False)
```

time: 597 us -> 282 us (0.47)
  waiting for transfers between devices: 300 us -> 146 us
  local copies, waits for them, and re-layouts: 158 us -> 17.2 us
  matrix products: 98.8 us -> 0.88 us
  Pallas kernels: 0 us -> 75.6 us
    psum x2 -> x1, waiting for transfers between devices: 220 us -> 118 us  [local(): dw_all = lax.psum(dw, ('row', 'col'))]
    dot_general x40 -> x2, matrix products: 98.8 us -> 0.88 us  [the longest x1 0.52 us: nt(): lax.dot_general(a, b, (((1,), (1,)), ((), ())), preferred_element_type=F32)]
    convert_element_type x13 -> x0, local copies, waits for them, and re-layouts: 76.2 us -> none  [the longest x6 51.9 us: block_step(): outer_grad.astype(jnp.bfloat16).reshape(IBLK, col_span, hidden, hidden)]
    pallas_call x0 -> x3, Pallas kernels: none -> 75.6 us  [the longest x1 31.8 us: local(): pl.pallas_call(functools.partial(grad_kernel, ib, seqs, hidden), grid=(st...]
    all_gather x1, waiting for transfers between devices: 55.1 us -> 3.3 us  [local(): right_cols = lax.all_gather(mine, 'row', axis=0, tiled=True)]
    while x37 -> x0, local copies, waits for them, and re-layouts: 47.6 us -> none
    dynamic_update_slice x12 -> x0, local copies, waits for them, and re-layouts: 17 us -> none  [local(): lax.scan(block_step, initial, (row_blocks, grad_blocks))]
    reshape x6 -> x13, local copies, waits for them, and re-layouts: 3.73 us -> 11.2 us  [the longest x1 2.72 us: local(): dl.reshape(rows, seqs * hidden)]
  transfers between devices with their start and end apart: 5 -> 6, of which waited for: 5 -> 3; matrix products, arithmetic and copies ran while one was open for 2% -> 7% of each run, Pallas kernels for 0% -> 27%
where the time goes in v1:
time: 282 us; the launch traced here: 281 us
  waiting for transfers between devices  146 us (52%)
  Pallas kernels  75.6 us (27%)
  local copies, waits for them, and re-layouts  17.2 us (6%)
  blocking collectives  16.1 us (6%)
  between operations  14.1 us (5%)
  other arithmetic  8.23 us (3%)
    psum x1, waiting for transfers between devices, local(): dw_all = lax.psum(dw, ('row', 'col'))  118 us
    pallas_call x1, Pallas kernels, local(): pl.pallas_call(functools.partial(grad_kernel, ib, seqs, hidden), grid=(st...  31.8 us
    reduce_scatter x1, waiting for transfers between devices, local(): dr_mine = lax.psum_scatter(dr, 'row', scatter_dimension=0, tiled=True)  24.9 us
    pallas_call x1, Pallas kernels, local(): pl.pallas_call(functools.partial(mix_kernel, ib, seqs, hidden), grid=(ste...  24.7 us
    pallas_call x1, Pallas kernels, local(): pl.pallas_call(functools.partial(update_kernel, ib), grid=(steps,), in_sp...  19.1 us
    all_gather x1, blocking collectives, local(): lax.all_gather(left.transpose(1, 0, 2), 'col', axis=0, tiled=True)  16.1 us
  transfers between devices with their start and end apart: 6, of which 3 were waited for; matrix products, arithmetic and copies ran while one was open for 7% of the time, Pallas kernels for 27%

profile of v1, /device:TPU:0, one launch (start us, length us, event | category | flops | bytes accessed | tf_op | source)
XLA Modules:
  0.0 281.0 jit_solution(14212559565649161675)
XLA Ops:
  7.3 1.5 convert_reduce_fusion
  8.8 1.6 fusion.11
  10.5 0.5 fusion.6
  11.0 0.4 fusion.19
  11.5 0.8 reshape.79
  12.5 0.7 collective-permute-start
  13.2 0.6 copy-done.4
  13.9 0.8 reshape.81
  14.7 0.3 copy.24
  15.1 16.1 %all_gather.7 = bf16[48,64,32]{1,2,0:T(8,128)(2,1)S(1)} all-gather(bf16[24,64,32]{1,2,0:T(8,128)(2,1)S(1)} %copy.24), channel_id=1, replica_groups=mesh['row'=16,'col'=2] {'col'}, dimensions={0}, use_global_device_ids=true | all-gather | bytes 294912 | tf_op jit(solution)/shard_map/all_gather | solution.py:114
  31.8 1.2 copy.26.l_ref
  33.0 0.7 broadcast_multiply_fusion.w_ref
  33.7 24.7 %mix.1 = (bf16[2048,6144]{1,0:T(8,128)(2,1)}, bf16[384,2048]{1,0:T(8,128)(2,1)}) custom-call(bf16[3072,32]{1,0:T(8,128)(2,1)} %copy.26.l_ref, bf16[32,4096]{1,0:T(8,128)(2,1)} %broadcast_multiply_fusion.w_ref, bf16[48,384,128]{2,1,0:T(8,128)(2,1)} %dp_ref.3), custom_call_target="tpu_custom_call" | custom-call | flops 9663676416 | bytes 30000000 | tf_op jit(solution)/shard_map/mix/pallas_call | solution.py:128
  58.5 1.3 copy.28
  59.8 3.3 %all-gather.2.cloned.1.call-done.r_ref = bf16[384,2048]{1,0:T(8,128)(2,1)} async-done(((bf16[24,2048]{1,0:T(8,128)(2,1)}), bf16[384,2048]{1,0:T(8,128)(2,1)}) %all-gather.2.cloned.1.call-update) | async-done | bytes 1572880 | tf_op jit(solution)/shard_map/all_gather | solution.py:120
  63.1 1.9 copy.27
  65.0 1.3 multiply_bitcast_fusion.rt_ref
  66.3 31.8 %grad.1 = (bf16[3072,32]{1,0:T(8,128)(2,1)}, f32[32,4096]{1,0:T(8,128)}) custom-call(bf16[2048,384]{1,0:T(8,128)(2,1)} %multiply_bitcast_fusion.rt_ref, bf16[48,384,128]{2,1,0:T(8,128)(2,1)} %dp_ref.3, bf16[4096,32]{1,0:T(8,128)(2,1)} %bitcast.35, bf16[32,3072]{1,0:T(8,128)(2,1)} %bitcast.36), custom_call_target="tpu_custom_call" | custom-call | flops 9663676416 | bytes 10000000 | tf_op jit(solution)/shard_map/grad/pallas_call | solution.py:153
  98.1 2.7 reshape.85
  100.9 24.9 %reduce-scatter.5.cloned.1.call-done = bf16[24,2048]{1,0:T(8,128)(2,1)} async-done(((bf16[384,2048]{1,0:T(8,128)(2,1)}), bf16[24,2048]{1,0:T(8,128)(2,1)}) %reduce-scatter.5.cloned.1.call-update) | async-done | bytes 98320 | tf_op jit(solution)/shard_map/reduce_scatter | solution.py:150
  125.8 1.5 collective-permute-start.1
  127.6 0.7 reshape.89
  128.4 0.9 reshape.91
  129.3 19.1 %update.1 = bf16[48,384,128]{2,1,0:T(8,128)(2,1)} custom-call(bf16[384,2048]{1,0:T(8,128)(2,1)} %all-gather.2.cloned.1.call-done.r_ref, bf16[2048,6144]{1,0:T(8,128)(2,1)} %get-tuple-element.7.m_ref, f32[1,128]{1,0:T(1,128)} %bitcast.37), custom_call_target="tpu_custom_call" | custom-call | flops 9663676416 | bytes 30000000 | tf_op jit(solution)/shard_map/update/pallas_call | solution.py:181
  148.4 1.2 reshape.86
  149.6 1.0 copy.29
  150.6 0.7 reshape.87
  151.3 0.5 multiply_reduce_fusion
  151.9 0.7 fusion.7
  152.7 1.7 fusion.10
  154.4 118.1 %all-reduce.2.cloned.1.call-done = f32[1024,128]{1,0:T(8,128)} async-done(((f32[1024,128]{1,0:T(8,128)}), f32[1024,128]{1,0:T(8,128)}) %all-reduce.2.cloned.1.call-update) | async-done | bytes 524304 | tf_op jit(solution)/shard_map/psum | solution.py:179
  272.6 1.9 copy.34
  (45 shorter events, 1.5 us)
Async XLA Ops:
  7.2 3.3 %copy-start = (bf16[64,24,256]{2,1,0:T(8,128)(2,1)S(1)}, bf16[64,24,256]{2,1,0:T(8,128)(2,1)}, u32[]{:S(2)}) copy-start(bf16[64,24,256]{2,1,0:T(8,128)(2,1)} %param.10) | copy-start | bytes 2359300
  7.2 3.3 %copy-start.6 = (bf16[256,32]{0,1:T(8,128)(2,1)S(1)}, bf16[256,32]{0,1:T(8,128)(2,1)}, u32[]{:S(2)}) copy-start(bf16[256,32]{0,1:T(8,128)(2,1)} %param.13) | copy-start | bytes 49156
  7.2 3.3 %copy-start.7 = (bf16[256,32]{0,1:T(8,128)(2,1)S(1)}, bf16[256,32]{0,1:T(8,128)(2,1)}, u32[]{:S(2)}) copy-start(bf16[256,32]{0,1:T(8,128)(2,1)} %param.15) | copy-start | bytes 49156
  7.2 3.3 %copy-start.5 = (f32[256]{0:T(256)S(1)}, f32[256]{0:T(256)}, u32[]{:S(2)}) copy-start(f32[256]{0:T(256)} %param.11) | copy-start | bytes 3076
  7.2 3.3 %copy-start.8 = (f32[256]{0:T(256)S(1)}, f32[256]{0:T(256)}, u32[]{:S(2)}) copy-start(f32[256]{0:T(256)} %param.12) | copy-start | bytes 3076
  7.2 55.9 %all-gather.2.cloned.1.call-start = ((), (), s32[]{:S(2)}) async-start(), calls=%async_computation.2 | async-start | bytes 1671168 | tf_op jit(solution)/shard_map/all_gather | solution.py:120
  10.4 1.0 copy-start.9
  10.4 1.0 copy-start.10
  12.5 0.7 collective-permute-start
  13.2 0.6 copy-start.4
  13.8 112.0 %reduce-scatter.5.cloned.1.call-start = ((), (), s32[]{:S(2)}) async-start(), calls=%async_computation.4 | async-start | bytes 1671168 | tf_op jit(solution)/shard_map/reduce_scatter | solution.py:150
  13.9 17.8 %copy-start.3 = (bf16[1024,128]{1,0:T(8,128)(2,1)S(1)}, bf16[1024,128]{1,0:T(8,128)(2,1)}, u32[]{:S(2)}) copy-start(bf16[1024,128]{1,0:T(8,128)(2,1)} %param.17) | copy-start | bytes 786436
  31.7 26.7 %copy-start.1 = (bf16[3072,32]{0,1:T(8,128)(2,1)}, bf16[3072,32]{0,1:T(8,128)(2,1)S(1)}, u32[]{:S(2)}) copy-start(bf16[3072,32]{0,1:T(8,128)(2,1)S(1)} %reshape.82) | copy-start | bytes 589828
  58.4 90.0 %reduce-scatter.3.cloned.1.call-start = ((), (), s32[]{:S(2)}) async-start(), calls=%async_computation.3 | async-start | bytes 294912 | tf_op jit(solution)/shard_map/reduce_scatter | solution.py:176
  98.1 30.3 %copy-start.2 = (f32[32,4096]{1,0:T(8,128)S(1)}, f32[32,4096]{1,0:T(8,128)}, u32[]{:S(2)}) copy-start(f32[32,4096]{1,0:T(8,128)} %get-tuple-element.10) | copy-start | bytes 1572868
  100.8 171.7 %all-reduce.2.cloned.1.call-start = ((), (), s32[]{:S(2)}) async-start(), calls=%async_computation.5 | async-start | bytes 1048576 | tf_op jit(solution)/shard_map/psum | solution.py:179
  125.8 1.5 collective-permute-start.1
Sparse Core Ops, SparseCore 0:
  14.0 49.1 all-gather.1
  67.4 58.4 reduce-scatter.4
  128.1 9.9 reduce-scatter.2
  144.7 127.8 all-reduce.1

commit v2 on v1

v2 whole, which is shorter than its diff:
```python
import functools

import jax
import jax.numpy as jnp
from jax import lax
from jax.experimental import pallas as pl
from jax.experimental.pallas import tpu as pltpu
from jax.sharding import PartitionSpec as P

BF = jnp.bfloat16
F32 = jnp.float32
MESH = pl.DeviceIdType.MESH


def divisor_up_to(total, most):
    best = 1
    for d in range(1, most + 1):
        if total % d == 0:
            best = d
    return best


def nn(a, b):
    return lax.dot_general(a, b, (((1,), (0,)), ((), ())), preferred_element_type=F32)


def nt(a, b):
    return lax.dot_general(a, b, (((1,), (1,)), ((), ())), preferred_element_type=F32)


def greet_all(me, ncol, total):
    barrier = pltpu.get_barrier_semaphore()

    def hello(k, carry):
        other = lax.rem(me + k, total)
        pl.semaphore_signal(barrier, inc=1, device_id=(other // ncol, lax.rem(other, ncol)), device_id_type=MESH)
        return carry

    lax.fori_loop(1, total, hello, 0)
    pl.semaphore_wait(barrier, total - 1)


def place(sizes):
    nrow, ncol = sizes
    r, c = lax.axis_index("row"), lax.axis_index("col")
    return r, c, r * ncol + c


def remote(src, dst, send, recv, row, col):
    return pltpu.make_async_remote_copy(
        src_ref=src, dst_ref=dst, send_sem=send, recv_sem=recv, device_id=(row, col), device_id_type=MESH
    )


def mix_kernel(sizes, ib, seqs, hidden, lt_ref, r_ref, w_ref, dp_ref, m_ref, dr_ref, ltall_ref, rall_ref,
               acc, wide, lbuf, lall, rbuf, lsend, lrecv, rsend, rrecv, fsend, own_sem):
    nrow, ncol = sizes
    half = nrow // 2
    r, c, me = place(sizes)
    step = pl.program_id(0)
    last = pl.num_programs(0) - 1
    out = dp_ref.shape[2]
    own, span = r_ref.shape[0], lt_ref.shape[1]
    par = lax.rem(r, 2)
    sib = r + 1 - 2 * par
    slot, block = lax.rem(me, nrow), me // nrow
    spar = lax.rem(slot, 2)

    def left_to(k):
        to = lax.rem(c + k, ncol)
        return remote(lt_ref, lbuf.at[c], lsend.at[k], lrecv.at[c], r, to)

    def left_from(k):
        fr = lax.rem(c + k, ncol)
        return remote(lt_ref, lbuf.at[fr], lsend.at[k], lrecv.at[fr], r, fr)

    def right_to(k):
        return remote(r_ref, rbuf.at[slot], rsend.at[k], rrecv.at[slot], 2 * k + spar, block)

    def is_me(k):
        return (block == c) & (2 * k + spar == r)

    def right_from(s):
        return remote(r_ref, rbuf.at[s], rsend.at[0], rrecv.at[s], sib, c)

    def forward(k):
        s = 2 * k + par
        return remote(rbuf.at[s], rbuf.at[s], fsend.at[k], rrecv.at[s], sib, c)

    keep = pltpu.make_async_copy(r_ref, rbuf.at[slot], own_sem)

    @pl.when(step == 0)
    def _():
        acc[...] = jnp.zeros_like(acc)
        greet_all(me, ncol, nrow * ncol)
        for k in range(1, ncol):
            left_to(k).start()
        for k in range(half):
            @pl.when(is_me(k))
            def _():
                keep.start()

            @pl.when(jnp.logical_not(is_me(k)))
            def _():
                right_to(k).start()
        lbuf[c] = lt_ref[...]
        for k in range(1, ncol):
            left_from(k).wait_recv()
        for k in range(ncol):
            ltall_ref[:, k * span : (k + 1) * span] = lbuf[k]
            lall[k * span : (k + 1) * span, :] = lbuf[k].astype(F32).T.astype(BF)

    rows = lall[pl.ds(pl.multiple_of(step * (ib * seqs), ib * seqs), ib * seqs), :]
    for q in range(0, hidden, 2):
        res = nn(rows, w_ref[:, q * out : (q + 2) * out]).astype(BF)
        for e in range(2):
            for i in range(ib):
                m_ref[(q + e) * seqs : (q + e + 1) * seqs, i * out : (i + 1) * out] = res[
                    i * seqs : (i + 1) * seqs, e * out : (e + 1) * out
                ]
    for i in range(ib):
        wide[:, i * out : (i + 1) * out] = dp_ref[i]
    width = 256
    for w in range(0, hidden * seqs, width):
        acc[:, w : w + width] += nt(wide[...], m_ref[w : w + width, :])

    @pl.when(step == last - 1)
    def _():
        for k in range(half):
            mine = c * nrow + 2 * k + par == me

            @pl.when(mine)
            def _():
                keep.wait()

            @pl.when(jnp.logical_not(mine))
            def _():
                right_from(2 * k + par).wait_recv()

            forward(k).start()

    @pl.when(step == last)
    def _():
        for k in range(nrow):
            dr_ref[k // 2, k % 2] = acc[k * own : (k + 1) * own, :].astype(BF)
        for k in range(half):
            right_from(2 * k + 1 - par).wait_recv()
            forward(k).wait_send()

            @pl.when(jnp.logical_not(is_me(k)))
            def _():
                right_to(k).wait_send()
        for k in range(1, ncol):
            left_to(k).wait_send()
        rall_ref[...] = rbuf[...]


def grad_kernel(sizes, ib, seqs, hidden, rt_ref, dp_ref, wt_ref, lt_ref, dr_ref, dl_ref, dw_ref, own_ref,
                nl, wide, mine, theirs, part, sum_sem, a_send, a_recv, b_send, b_recv, keep_sem):
    nrow, ncol = sizes
    half = nrow // 2
    r, c, me = place(sizes)
    step = pl.program_id(0)
    last = pl.num_programs(0) - 1
    out = dp_ref.shape[2]
    par = lax.rem(r, 2)
    sib = r + 1 - 2 * par
    slot, block = lax.rem(me, nrow), me // nrow
    spar = lax.rem(slot, 2)
    place_of = r // 2

    to_sib = remote(dr_ref.at[:, 1 - par], theirs, a_send, a_recv, sib, c)
    load = pltpu.make_async_copy(dr_ref.at[:, par], mine, sum_sem)

    def owner(k):
        g = c * nrow + 2 * k + par
        return g

    def to_owner(k):
        g = owner(k)
        return remote(mine.at[k], part.at[place_of], b_send.at[k], b_recv.at[place_of], g // ncol, lax.rem(g, ncol))

    def keep(k):
        return pltpu.make_async_copy(mine.at[k], part.at[place_of], keep_sem)

    def from_row(k):
        return remote(mine.at[0], part.at[k], b_send.at[0], b_recv.at[k], 2 * k + spar, block)

    @pl.when(step == 0)
    def _():
        greet_all(me, ncol, nrow * ncol)
        to_sib.start()
        load.start()
        dw_ref[...] = jnp.zeros_like(dw_ref)

    @pl.when(step == 1)
    def _():
        load.wait()
        to_sib.wait_recv()
        for k in range(half):
            mine[k] = (mine[k].astype(F32) + theirs[k].astype(F32)).astype(BF)
        for k in range(half):
            @pl.when(owner(k) == me)
            def _():
                keep(k).start()

            @pl.when(owner(k) != me)
            def _():
                to_owner(k).start()

    for i in range(ib):
        wide[:, i * out : (i + 1) * out] = dp_ref[i]
    qs = 4
    for q in range(0, hidden, qs):
        res = nn(rt_ref[q * seqs : (q + qs) * seqs, :], wide[...]).astype(BF)
        for e in range(qs):
            for i in range(ib):
                nl[i * seqs : (i + 1) * seqs, (q + e) * out : (q + e + 1) * out] = res[
                    e * seqs : (e + 1) * seqs, i * out : (i + 1) * out
                ]
    dl_ref[...] = nn(nl[...], wt_ref[...]).astype(BF)
    width = 512
    for w in range(0, hidden * out, width):
        dw_ref[:, w : w + width] += nn(lt_ref[...], nl[:, w : w + width])

    @pl.when(step == last)
    def _():
        to_sib.wait_send()
        for k in range(half):
            @pl.when(owner(k) == me)
            def _():
                keep(k).wait()

            @pl.when(owner(k) != me)
            def _():
                to_owner(k).wait_send()
        for k in range(half):
            @pl.when(jnp.logical_not((block == c) & (2 * k + spar == r)))
            def _():
                from_row(k).wait_recv()
        total = part[0].astype(F32)
        for k in range(1, half):
            total = total + part[k].astype(F32)
        own_ref[...] = total.astype(BF)


def update_kernel(sizes, ib, r_ref, m_ref, b_ref, dw_ref, dl_ref, o_ref, dwall_ref, dlown_ref,
                  wbuf, wsum, wall, lbuf, lsum, wsend, wrecv, gsend, grecv, lsend, lrecv, lkeep, wkeep):
    nrow, ncol = sizes
    total = nrow * ncol
    r, c, me = place(sizes)
    step = pl.program_id(0)
    last = pl.num_programs(0) - 1
    out = o_ref.shape[2]

    def scatter(k):
        to = lax.rem(me + k, total)
        return remote(dw_ref.at[to], wbuf.at[me], wsend.at[k], wrecv.at[me], to // ncol, lax.rem(to, ncol))

    def scattered(k):
        fr = lax.rem(me + k, total)
        return remote(dw_ref.at[fr], wbuf.at[fr], wsend.at[k], wrecv.at[fr], fr // ncol, lax.rem(fr, ncol))

    def gather(k):
        to = lax.rem(me + k, total)
        return remote(wsum, wall.at[me], gsend.at[k], grecv.at[me], to // ncol, lax.rem(to, ncol))

    def gathered(k):
        fr = lax.rem(me + k, total)
        return remote(wsum, wall.at[fr], gsend.at[k], grecv.at[fr], fr // ncol, lax.rem(fr, ncol))

    def left_to(k):
        to = lax.rem(c + k, ncol)
        return remote(dl_ref.at[to], lbuf.at[c], lsend.at[k], lrecv.at[c], r, to)

    def left_from(k):
        fr = lax.rem(c + k, ncol)
        return remote(dl_ref.at[fr], lbuf.at[fr], lsend.at[k], lrecv.at[fr], r, fr)

    own_left = pltpu.make_async_copy(dl_ref.at[c], lbuf.at[c], lkeep)
    own_w = pltpu.make_async_copy(dw_ref.at[me], wbuf.at[me], wkeep)

    def every(act):
        def body(k, carry):
            act(k)
            return carry

        lax.fori_loop(1, total, body, 0)

    @pl.when(step == 0)
    def _():
        own_left.start()
        own_w.start()
        greet_all(me, ncol, total)
        every(lambda k: scatter(k).start())
        for k in range(1, ncol):
            left_to(k).start()

    @pl.when(step == pl.num_programs(0) // 2)
    def _():
        own_w.wait()
        every(lambda k: scattered(k).wait_recv())
        wsum[...] = jnp.sum(wbuf[...].astype(F32), axis=0).astype(BF)
        wall[me] = wsum[...]
        every(lambda k: gather(k).start())

    for i in range(0, ib, 2):
        res = nn(r_ref[...], m_ref[:, i * out : (i + 2) * out])
        for e in range(2):
            o_ref[i + e] = (res[:, e * out : (e + 1) * out] + b_ref[...]).astype(BF)

    @pl.when(step == last)
    def _():
        own_left.wait()
        for k in range(1, ncol):
            left_from(k).wait_recv()
            left_to(k).wait_send()
        got = lbuf[0].astype(F32)
        for k in range(1, ncol):
            got = got + lbuf[k].astype(F32)
        dlown_ref[...] = got.astype(BF)
        every(lambda k: scatter(k).wait_send())
        every(lambda k: gathered(k).wait_recv())
        every(lambda k: gather(k).wait_send())
        dwall_ref[...] = wall[...]


def apply_layer_norm(x, gain, bias):
    v = x.astype(F32)
    average = jnp.mean(v, axis=-1, keepdims=True)
    shifted = v - average
    variance = jnp.mean(shifted * shifted, axis=-1, keepdims=True)
    inv = lax.rsqrt(variance + 1e-05)
    standard = shifted * inv
    return standard, inv, (standard * gain + bias).astype(BF)


def local(x, gain, bias, wl, bl, wr, br, wo, bo, dp):
    seqs, own, width = x.shape
    hidden = wl.shape[1]
    out = wo.shape[1]
    nrow, ncol = lax.axis_size("row"), lax.axis_size("col")
    sizes = (nrow, ncol)
    total = nrow * ncol
    half = nrow // 2
    rows, cols, _ = dp.shape
    qs = hidden * seqs
    qh = hidden * out
    factor = 1.0 / seqs

    standard, inv, normed = apply_layer_norm(x, gain, bias)
    both = nn(normed.reshape(-1, width), jnp.concatenate([wl, wr], axis=1))
    left = (both[:, :hidden] + bl).astype(BF).reshape(seqs, own, hidden)
    right = (both[:, hidden:] + br).astype(BF).reshape(seqs, own, hidden)
    left_t = left.transpose(2, 1, 0).reshape(hidden, own * seqs)
    right_own = right.transpose(1, 2, 0).reshape(own, qs)

    w2 = wo.reshape(hidden, qh)
    ib = divisor_up_to(rows, 4)
    steps = rows // ib
    dma = pltpu.SemaphoreType.DMA
    anywhere = pl.BlockSpec(memory_space=pl.ANY)

    def params(n):
        return pltpu.CompilerParams(
            vmem_limit_bytes=56 * 1024 * 1024, collective_id=n, has_side_effects=True
        )

    cost = pl.CostEstimate(flops=2 * cols * qs * rows * out, bytes_accessed=30000000, transcendentals=0)

    def whole(*shape):
        return pl.BlockSpec(shape, lambda t: (0,) * len(shape))

    m, dr, left_all, right_slots = pl.pallas_call(
        functools.partial(mix_kernel, sizes, ib, seqs, hidden),
        grid=(steps,),
        in_specs=[
            whole(hidden, own * seqs),
            whole(own, qs),
            whole(hidden, qh),
            pl.BlockSpec((ib, cols, out), lambda t: (t, 0, 0)),
        ],
        out_specs=[
            pl.BlockSpec((qs, ib * out), lambda t: (0, t)),
            whole(half, 2, own, qs),
            whole(hidden, rows * seqs),
            whole(nrow, own, qs),
        ],
        out_shape=[
            jax.ShapeDtypeStruct((qs, rows * out), BF),
            jax.ShapeDtypeStruct((half, 2, own, qs), BF),
            jax.ShapeDtypeStruct((hidden, rows * seqs), BF),
            jax.ShapeDtypeStruct((nrow, own, qs), BF),
        ],
        scratch_shapes=[
            pltpu.VMEM((cols, qs), F32),
            pltpu.VMEM((cols, ib * out), BF),
            pltpu.VMEM((ncol, hidden, own * seqs), BF),
            pltpu.VMEM((rows * seqs, hidden), BF),
            pltpu.VMEM((nrow, own, qs), BF),
            dma((ncol,)),
            dma((ncol,)),
            dma((half,)),
            dma((nrow,)),
            dma((half,)),
            dma,
        ],
        compiler_params=params(1),
        cost_estimate=cost,
        name="mix",
    )(left_t, right_own, w2 * BF(factor), dp)

    right_cols = right_slots.reshape(cols, qs)
    right_t = (right_cols * BF(factor)).T

    dl, dw, dr_own = pl.pallas_call(
        functools.partial(grad_kernel, sizes, ib, seqs, hidden),
        grid=(steps,),
        in_specs=[
            whole(qs, cols),
            pl.BlockSpec((ib, cols, out), lambda t: (t, 0, 0)),
            whole(qh, hidden),
            pl.BlockSpec((hidden, ib * seqs), lambda t: (0, t)),
            anywhere,
        ],
        out_specs=[
            pl.BlockSpec((ib * seqs, hidden), lambda t: (t, 0)),
            whole(hidden, qh),
            whole(own, qs),
        ],
        out_shape=[
            jax.ShapeDtypeStruct((rows * seqs, hidden), BF),
            jax.ShapeDtypeStruct((hidden, qh), F32),
            jax.ShapeDtypeStruct((own, qs), BF),
        ],
        scratch_shapes=[
            pltpu.VMEM((ib * seqs, qh), BF),
            pltpu.VMEM((cols, ib * out), BF),
            pltpu.VMEM((half, own, qs), BF),
            pltpu.VMEM((half, own, qs), BF),
            pltpu.VMEM((half, own, qs), BF),
            dma,
            dma,
            dma,
            dma((half,)),
            dma((half,)),
            dma,
        ],
        compiler_params=params(2),
        cost_estimate=cost,
        name="grad",
    )(right_t, dp, w2.T, left_all, dr)

    share = hidden * hidden // total
    dw3 = dw.astype(BF).reshape(total, share, out)
    dl3 = dl.reshape(ncol, own, seqs * hidden)
    update, dw_all, dl_own = pl.pallas_call(
        functools.partial(update_kernel, sizes, ib),
        grid=(steps,),
        in_specs=[
            whole(cols, qs),
            pl.BlockSpec((qs, ib * out), lambda t: (0, t)),
            whole(1, out),
            anywhere,
            anywhere,
        ],
        out_specs=[
            pl.BlockSpec((ib, cols, out), lambda t: (t, 0, 0)),
            whole(total, share, out),
            whole(own, seqs * hidden),
        ],
        out_shape=[
            jax.ShapeDtypeStruct((rows, cols, out), BF),
            jax.ShapeDtypeStruct((total, share, out), BF),
            jax.ShapeDtypeStruct((own, seqs * hidden), BF),
        ],
        scratch_shapes=[
            pltpu.VMEM((total, share, out), BF),
            pltpu.VMEM((share, out), BF),
            pltpu.VMEM((total, share, out), BF),
            pltpu.VMEM((ncol, own, seqs * hidden), BF),
            pltpu.VMEM((8, 128), F32),
            dma((total,)),
            dma((total,)),
            dma((total,)),
            dma((total,)),
            dma((ncol,)),
            dma((ncol,)),
            dma,
            dma,
        ],
        compiler_params=params(3),
        cost_estimate=cost,
        name="update",
    )(right_cols, m, bo.reshape(1, out), dw3, dl3)

    dl4 = dl_own.reshape(own, seqs, hidden).transpose(1, 0, 2).reshape(-1, hidden)
    dr4 = dr_own.reshape(own, hidden, seqs).transpose(2, 0, 1).reshape(-1, hidden)
    g = nt(jnp.concatenate([dl4, dr4], axis=1), jnp.concatenate([wl, wr], axis=1))
    g = g.reshape(seqs, own, width) * gain
    centre = jnp.mean(g, axis=-1, keepdims=True)
    slope = jnp.mean(g * standard, axis=-1, keepdims=True)
    dx = (inv * (g - centre - standard * slope)).astype(BF)
    return update, dx, dw_all.astype(F32).reshape(hidden * hidden, out)


def solution(mesh):
    both = ("row", "col")
    in_specs = (P(None, both, None),) + (P(),) * 8 + (P("row", "col", None),)
    out_specs = (P("row", "col", None), P(None, both, None), P())
    return jax.shard_map(local, mesh=mesh, in_specs=in_specs, out_specs=out_specs, check_vma=False)
```

time: 282 us -> 144 us (0.51)
  waiting for transfers between devices: 146 us -> 0 us
  Pallas kernels: 75.6 us -> 113 us
  blocking collectives: 16.1 us -> 0 us
  between operations: 14.1 us -> 0.94 us
    psum x1 -> x0, waiting for transfers between devices: 118 us -> none  [local(): dw_all = lax.psum(dw, ('row', 'col'))]
    pallas_call x3, Pallas kernels: 75.6 us -> 113 us  [the longest x1 40.8 us: local(): pl.pallas_call(functools.partial(mix_kernel, sizes, ib, seqs, hidden), gr...]
    reduce_scatter x2 -> x0, waiting for transfers between devices: 24.9 us -> none  [the longest x1 24.9 us: local(): dr_mine = lax.psum_scatter(dr, 'row', scatter_dimension=0, tiled=True)]
    all_gather x1 -> x0, blocking collectives: 16.1 us -> none  [local(): lax.all_gather(left.transpose(1, 0, 2), 'col', axis=0, tiled=True)]
    unnamed x24 -> x25, local copies, waits for them, and re-layouts: 2.55 us -> 5.85 us
    all_gather x1 -> x0, waiting for transfers between devices: 3.3 us -> none  [local(): right_cols = lax.all_gather(mine, 'row', axis=0, tiled=True)]
  transfers between devices with their start and end apart: 6 -> 0, of which waited for: 3 -> 0; matrix products, arithmetic and copies ran while one was open for 7% -> 0% of each run, Pallas kernels for 27% -> 0%
where the time goes in v2:
time: 144 us
  Pallas kernels  113 us (78%)
  local copies, waits for them, and re-layouts  17.9 us (12%)
  other arithmetic  10.4 us (7%)
    pallas_call x1, Pallas kernels, local(): pl.pallas_call(functools.partial(mix_kernel, sizes, ib, seqs, hidden), gr...  40.8 us
    pallas_call x1, Pallas kernels, local(): pl.pallas_call(functools.partial(update_kernel, sizes, ib), grid=(steps,)...  38.3 us
    pallas_call x1, Pallas kernels, local(): pl.pallas_call(functools.partial(grad_kernel, sizes, ib, seqs, hidden), g...  34.4 us
    unnamed x25, local copies, waits for them, and re-layouts  5.85 us

profile of v2, /device:TPU:0, one launch (start us, length us, event | category | flops | bytes accessed | tf_op | source)
XLA Modules:
  0.0 143.5 jit_solution(2254158676034758975)
XLA Ops:
  0.7 1.5 %convert_reduce_fusion = f32[64,24]{1,0:T(8,128)S(1)} fusion(bf16[64,24,256]{2,1,0:T(8,128)(2,1)} %param.10), kind=kLoop, calls=%fused_computation.1 | loop fusion | flops 784896 | bytes 792576 | tf_op jit(solution)/shard_map/reduce_sum | solution.py:330
  2.2 1.6 %fusion.11 = f32[64,24]{1,0:T(8,128)S(1)} fusion(bf16[64,24,256]{2,1,0:T(8,128)(2,1)} %param.10, f32[64,24]{1,0:T(8,128)S(1)} %broadcast_multiply_fusion.2), kind=kLoop, calls=%fused_computation.13 | loop fusion | flops 1571328 | bytes 798720 | tf_op jit(solution)/shard_map/reduce_sum | solution.py:332
  3.9 0.5 fusion.6
  4.4 0.4 fusion.19
  4.8 0.1 fusion.12
  4.9 0.8 reshape.88
  5.7 0.2 copy.17
  5.9 0.8 reshape.89.lt_ref
  6.8 0.8 reshape.90
  7.6 0.8 copy.23.r_ref
  8.4 0.1 reshape.92
  8.5 0.7 broadcast_multiply_fusion.w_ref
  9.3 40.8 %mix.1 = (bf16[2048,6144]{1,0:T(8,128)(2,1)}, bf16[8,2,24,2048]{3,2,1,0:T(8,128)(2,1)}, bf16[32,3072]{1,0:T(8,128)(2,1)}, bf16[16,24,2048]{2,1,0:T(8,128)(2,1)}) custom-call(bf16[32,1536]{1,0:T(8,128)(2,1)} %reshape.89.lt_ref, bf16[24,2048]{1,0:T(8,128)(2,1)} %copy.23.r_ref, bf16[32,4096]{1,0:T(8,128)(2,1)} %broadcast_multiply_fusion.w_ref, ...), custom_call_target="tpu_custom_call" | custom-call | flops 9663676416 | bytes 30000000 | tf_op jit(solution)/shard_map/mix/pallas_call | solution.py:374
  50.0 1.5 %multiply_bitcast_fusion = bf16[2048,384]{0,1:T(8,128)(2,1)S(1)} fusion(bf16[16,24,2048]{2,1,0:T(8,128)(2,1)} %get-tuple-element.13), kind=kLoop, calls=%fused_computation.15 | loop fusion | flops 786432 | bytes 3145728 | tf_op jit(solution)/shard_map/transpose | solution.py:414
  51.6 1.6 %copy.20.rt_ref = bf16[2048,384]{1,0:T(8,128)(2,1)} copy(bf16[2048,384]{0,1:T(8,128)(2,1)S(1)} %multiply_bitcast_fusion) | data formatting | bytes 3145728 | tf_op jit(solution)/shard_map/transpose | solution.py:414
  53.1 1.3 copy.19
  54.5 34.4 %grad.1 = (bf16[3072,32]{1,0:T(8,128)(2,1)}, f32[32,4096]{1,0:T(8,128)}, bf16[24,2048]{1,0:T(8,128)(2,1)}) custom-call(bf16[2048,384]{1,0:T(8,128)(2,1)} %copy.20.rt_ref, bf16[48,384,128]{2,1,0:T(8,128)(2,1)} %dp_ref.3, bf16[4096,32]{1,0:T(8,128)(2,1)} %bitcast.41, bf16[32,3072]{1,0:T(8,128)(2,1)} %get-tuple-element.15.lt_ref, ...), custom_call_target="tpu_custom_call" | custom-call | flops 9663676416 | bytes 30000000 | tf_op jit(solution)/shard_map/grad/pallas_call | solution.py:416
  88.9 1.2 convert_bitcast_fusion
  90.1 0.7 copy.25
  90.8 1.5 %reshape.96.dl_ref = bf16[2,24,2048]{2,1,0:T(8,128)(2,1)} reshape(bf16[3072,32]{1,0:T(8,128)(2,1)S(1)} %copy-done.1) | data formatting | bytes 393216 | tf_op jit(solution)/shard_map/reshape | solution.py:456
  92.3 38.3 %update.1 = (bf16[48,384,128]{2,1,0:T(8,128)(2,1)}, bf16[32,32,128]{2,1,0:T(8,128)(2,1)}, bf16[24,2048]{1,0:T(8,128)(2,1)}) custom-call(bf16[384,2048]{1,0:T(8,128)(2,1)} %bitcast.39, bf16[2048,6144]{1,0:T(8,128)(2,1)} %get-tuple-element.14.m_ref, f32[1,128]{1,0:T(1,128)} %bitcast.43, bf16[32,32,128]{2,1,0:T(8,128)(2,1)} %bitcast.42, ...), custom_call_target="tpu_custom_call" | custom-call | flops 9663676416 | bytes 30000000 | tf_op jit(solution)/shard_map/update/pallas_call | solution.py:457
  130.7 0.3 copy.24
  130.9 0.7 reshape.100
  131.6 1.2 reshape.97
  132.9 1.0 copy.21
  133.8 0.7 reshape.98
  134.5 0.5 multiply_reduce_fusion
  135.1 0.7 fusion.7
  135.8 0.1 div.17
  135.9 1.7 %fusion.10 = bf16[64,24,256]{2,1,0:T(8,128)(2,1)} fusion(bf16[64,24,256]{2,1,0:T(8,128)(2,1)S(1)} %copy-done, f32[64,24,256]{2,1,0:T(8,128)S(1)} %bitcast.34, f32[64,24]{1,0:T(8,128)S(1)} %broadcast_multiply_fusion.1, f32[64,24]{1,0:T(8,128)S(1)} %div.17, f32[256]{0:T(256)S(1)} %copy-done.5, f32[64,24]{1,0:T(8,128)S(1)} %add_rsqrt_fusion, ...), kind=kLoop, calls=%fused_computation.12 | loop fusion | flops 3538944 | bytes 3171328 | tf_op jit(solution)/shard_map/convert_element_type | solution.py:503
  137.6 0.8 bitcast_convert_fusion
  138.5 5.1 %copy.28 = bf16[48,384,128]{2,1,0:T(8,128)(2,1)} copy(bf16[48,384,128]{2,1,0:T(8,128)(2,1)} %get-tuple-element.30) | data formatting | bytes 9437184
  (28 shorter events, 0.1 us)
Async XLA Ops:
  0.6 3.2 %copy-start = (bf16[64,24,256]{2,1,0:T(8,128)(2,1)S(1)}, bf16[64,24,256]{2,1,0:T(8,128)(2,1)}, u32[]{:S(2)}) copy-start(bf16[64,24,256]{2,1,0:T(8,128)(2,1)} %param.10) | copy-start | bytes 2359300
  0.6 3.2 %copy-start.8 = (f32[256]{0:T(256)S(1)}, f32[256]{0:T(256)}, u32[]{:S(2)}) copy-start(f32[256]{0:T(256)} %param.12) | copy-start | bytes 3076
  0.7 3.2 %copy-start.5 = (f32[256]{0:T(256)S(1)}, f32[256]{0:T(256)}, u32[]{:S(2)}) copy-start(f32[256]{0:T(256)} %param.11) | copy-start | bytes 3076
  0.7 3.7 %copy-start.6 = (bf16[256,32]{0,1:T(8,128)(2,1)S(1)}, bf16[256,32]{0,1:T(8,128)(2,1)}, u32[]{:S(2)}) copy-start(bf16[256,32]{0,1:T(8,128)(2,1)} %param.13) | copy-start | bytes 49156
  0.7 3.7 %copy-start.7 = (bf16[256,32]{0,1:T(8,128)(2,1)S(1)}, bf16[256,32]{0,1:T(8,128)(2,1)}, u32[]{:S(2)}) copy-start(bf16[256,32]{0,1:T(8,128)(2,1)} %param.15) | copy-start | bytes 49156
  3.8 1.0 copy-start.9
  3.8 1.0 copy-start.10
  4.9 3.5 %copy-start.3 = (bf16[1024,128]{1,0:T(8,128)(2,1)S(1)}, bf16[1024,128]{1,0:T(8,128)(2,1)}, u32[]{:S(2)}) copy-start(bf16[1024,128]{1,0:T(8,128)(2,1)} %param.17) | copy-start | bytes 786436
  88.9 1.9 %copy-start.1 = (bf16[3072,32]{1,0:T(8,128)(2,1)S(1)}, bf16[3072,32]{1,0:T(8,128)(2,1)}, u32[]{:S(2)}) copy-start(bf16[3072,32]{1,0:T(8,128)(2,1)} %get-tuple-element.18) | copy-start | bytes 589828
  92.3 38.3 %copy-start.4 = (bf16[24,2048]{1,0:T(8,128)(2,1)S(1)}, bf16[24,2048]{1,0:T(8,128)(2,1)}, u32[]{:S(2)}) copy-start(bf16[24,2048]{1,0:T(8,128)(2,1)} %get-tuple-element.21) | copy-start | bytes 294916
  135.9 1.7 %copy-start.2 = (bf16[32,32,128]{2,1,0:T(8,128)(2,1)S(1)}, bf16[32,32,128]{2,1,0:T(8,128)(2,1)}, u32[]{:S(2)}) copy-start(bf16[32,32,128]{2,1,0:T(8,128)(2,1)} %get-tuple-element.22) | copy-start | bytes 786436

commit v3 on v1

v3 whole, which is shorter than its diff:
```python
import functools

import jax
import jax.numpy as jnp
from jax import lax
from jax.experimental import pallas as pl
from jax.experimental.pallas import tpu as pltpu
from jax.sharding import PartitionSpec as P

BF = jnp.bfloat16
F32 = jnp.float32
MESH = pl.DeviceIdType.MESH


def divisor_up_to(total, most):
    best = 1
    for d in range(1, most + 1):
        if total % d == 0:
            best = d
    return best


def nn(a, b):
    return lax.dot_general(a, b, (((1,), (0,)), ((), ())), preferred_element_type=F32)


def nt(a, b):
    return lax.dot_general(a, b, (((1,), (1,)), ((), ())), preferred_element_type=F32)


def greet_all(me, ncol, total):
    barrier = pltpu.get_barrier_semaphore()

    def hello(k, carry):
        other = lax.rem(me + k, total)
        pl.semaphore_signal(barrier, inc=1, device_id=(other // ncol, lax.rem(other, ncol)), device_id_type=MESH)
        return carry

    lax.fori_loop(1, total, hello, 0)
    pl.semaphore_wait(barrier, total - 1)


def place(sizes):
    nrow, ncol = sizes
    r, c = lax.axis_index("row"), lax.axis_index("col")
    return r, c, r * ncol + c


def remote(src, dst, send, recv, row, col):
    return pltpu.make_async_remote_copy(
        src_ref=src, dst_ref=dst, send_sem=send, recv_sem=recv, device_id=(row, col), device_id_type=MESH
    )


def pair_kernel(sizes, ib, seqs, hidden, lt_ref, r_ref, w_ref, wt_ref, b_ref, dp_ref, o_ref, dwall_ref, dlown_ref,
                drown_ref, m_all, acc, wide, nl, lbuf, ltall, lall, rbuf, rcols, rt, drbuf, theirs, part, dwacc, dw3,
                wbuf, wsum, wall, dlbuf, dlgot, lsend, lrecv, rsend, rrecv, fsend, a_send, a_recv, b_send, b_recv,
                wsend, wrecv, gsend, grecv, dsend, drecv, local_sem):
    nrow, ncol = sizes
    half = nrow // 2
    total = nrow * ncol
    r, c, me = place(sizes)
    steps = pl.num_programs(0) // 3
    t = pl.program_id(0)
    u = lax.rem(t, steps)
    out = dp_ref.shape[2]
    own, span = r_ref.shape[0], lt_ref.shape[1]
    qs, qh = hidden * seqs, hidden * out
    par = lax.rem(r, 2)
    sib = r + 1 - 2 * par
    slot, block = lax.rem(me, nrow), me // nrow
    spar = lax.rem(slot, 2)
    place_of = r // 2
    factor = 1.0 / seqs

    def left_to(k):
        to = lax.rem(c + k, ncol)
        return remote(lt_ref, lbuf.at[c], lsend.at[k], lrecv.at[c], r, to)

    def left_from(k):
        fr = lax.rem(c + k, ncol)
        return remote(lt_ref, lbuf.at[fr], lsend.at[k], lrecv.at[fr], r, fr)

    def right_to(k):
        return remote(r_ref, rbuf.at[slot], rsend.at[k], rrecv.at[slot], 2 * k + spar, block)

    def is_me(k):
        return (block == c) & (2 * k + spar == r)

    def right_from(s):
        return remote(r_ref, rbuf.at[s], rsend.at[0], rrecv.at[s], sib, c)

    def forward(k):
        s = 2 * k + par
        return remote(rbuf.at[s], rbuf.at[s], fsend.at[k], rrecv.at[s], sib, c)

    keep = pltpu.make_async_copy(r_ref, rbuf.at[slot], local_sem.at[0])
    to_sib = remote(drbuf.at[:, 1 - par], theirs, a_send, a_recv, sib, c)

    def owner(k):
        return c * nrow + 2 * k + par

    def to_owner(k):
        g = owner(k)
        return remote(theirs.at[k], part.at[place_of], b_send.at[k], b_recv.at[place_of], g // ncol, lax.rem(g, ncol))

    def keep_part(k):
        return pltpu.make_async_copy(theirs.at[k], part.at[place_of], local_sem.at[1])

    def from_row(k):
        return remote(theirs.at[0], part.at[k], b_send.at[0], b_recv.at[k], 2 * k + spar, block)

    def scatter(k):
        to = lax.rem(me + k, total)
        return remote(dw3.at[to], wbuf.at[me], wsend.at[k], wrecv.at[me], to // ncol, lax.rem(to, ncol))

    def scattered(k):
        fr = lax.rem(me + k, total)
        return remote(dw3.at[fr], wbuf.at[fr], wsend.at[k], wrecv.at[fr], fr // ncol, lax.rem(fr, ncol))

    def gather(k):
        to = lax.rem(me + k, total)
        return remote(wsum, wall.at[me], gsend.at[k], grecv.at[me], to // ncol, lax.rem(to, ncol))

    def gathered(k):
        fr = lax.rem(me + k, total)
        return remote(wsum, wall.at[fr], gsend.at[k], grecv.at[fr], fr // ncol, lax.rem(fr, ncol))

    def dl_piece(k):
        return dlbuf.at[pl.ds(pl.multiple_of(k * span, span), span), :]

    def dl_to(k):
        to = lax.rem(c + k, ncol)
        return remote(dl_piece(to), dlgot.at[c], dsend.at[k], drecv.at[c], r, to)

    def dl_from(k):
        fr = lax.rem(c + k, ncol)
        return remote(dl_piece(fr), dlgot.at[fr], dsend.at[k], drecv.at[fr], r, fr)

    def every(act):
        def body(k, carry):
            act(k)
            return carry

        lax.fori_loop(1, total, body, 0)

    @pl.when(t == 0)
    def _():
        greet_all(me, ncol, total)
        for k in range(1, ncol):
            left_to(k).start()
        for k in range(half):
            @pl.when(is_me(k))
            def _():
                keep.start()

            @pl.when(jnp.logical_not(is_me(k)))
            def _():
                right_to(k).start()
        acc[...] = jnp.zeros_like(acc)
        dwacc[...] = jnp.zeros_like(dwacc)
        lbuf[c] = lt_ref[...]
        for k in range(1, ncol):
            left_from(k).wait_recv()
        for k in range(ncol):
            ltall[:, k * span : (k + 1) * span] = lbuf[k]
            lall[k * span : (k + 1) * span, :] = lbuf[k].astype(F32).T.astype(BF)

    def spread():
        for i in range(ib):
            wide[:, i * out : (i + 1) * out] = dp_ref[i]

    @pl.when(t < steps)
    def _():
        m_ref = m_all.at[u]
        rows = lall[pl.ds(pl.multiple_of(u * (ib * seqs), ib * seqs), ib * seqs), :]
        for q in range(0, hidden, 2):
            res = nn(rows, w_ref[:, q * out : (q + 2) * out]).astype(BF)
            for e in range(2):
                for i in range(ib):
                    m_ref[(q + e) * seqs : (q + e + 1) * seqs, i * out : (i + 1) * out] = res[
                        i * seqs : (i + 1) * seqs, e * out : (e + 1) * out
                    ]
        spread()
        width = 256
        for w in range(0, qs, width):
            acc[:, w : w + width] += nt(wide[...], m_ref[w : w + width, :])

    @pl.when(t == steps - 1)
    def _():
        for k in range(half):
            mine = c * nrow + 2 * k + par == me

            @pl.when(mine)
            def _():
                keep.wait()

            @pl.when(jnp.logical_not(mine))
            def _():
                right_from(2 * k + par).wait_recv()

            forward(k).start()
        for k in range(nrow):
            drbuf[k // 2, k % 2] = acc[k * own : (k + 1) * own, :].astype(BF)
        to_sib.start()

    @pl.when(t == steps)
    def _():
        for k in range(half):
            right_from(2 * k + 1 - par).wait_recv()
        for k in range(nrow):
            acc[k * own : (k + 1) * own, :] = rbuf[k].astype(F32)
        width = 256
        for w in range(0, qs, width):
            piece = acc[:, w : w + width]
            rcols[:, w : w + width] = piece.astype(BF)
            rt[w : w + width, :] = (piece * factor).T.astype(BF)
        to_sib.wait_recv()
        for k in range(half):
            theirs[k] = (drbuf[k, par].astype(F32) + theirs[k].astype(F32)).astype(BF)
        for k in range(half):
            @pl.when(owner(k) == me)
            def _():
                keep_part(k).start()

            @pl.when(owner(k) != me)
            def _():
                to_owner(k).start()

    @pl.when((t >= steps) & (t < 2 * steps))
    def _():
        spread()
        group = 4
        for q in range(0, hidden, group):
            res = nn(rt[q * seqs : (q + group) * seqs, :], wide[...]).astype(BF)
            for e in range(group):
                for i in range(ib):
                    nl[i * seqs : (i + 1) * seqs, (q + e) * out : (q + e + 1) * out] = res[
                        e * seqs : (e + 1) * seqs, i * out : (i + 1) * out
                    ]
        here = pl.ds(pl.multiple_of(u * (ib * seqs), ib * seqs), ib * seqs)
        dlbuf[here, :] = nn(nl[...], wt_ref[...]).astype(BF)
        width = 512
        lt_here = ltall[:, here]
        for w in range(0, qh, width):
            dwacc[:, w : w + width] += nn(lt_here, nl[:, w : w + width])

    @pl.when(t == 2 * steps - 1)
    def _():
        share = dw3.shape[1]
        per = hidden // share
        for q in range(hidden):
            for e in range(per):
                dw3[q * per + e] = dwacc[e * share : (e + 1) * share, q * out : (q + 1) * out].astype(BF)
        every(lambda k: scatter(k).start())
        for k in range(1, ncol):
            dl_to(k).start()
        wbuf[me] = dw3[me]
        dlgot[c] = dl_piece(c)[...]

    @pl.when(t == 2 * steps + (steps * 5) // 12)
    def _():
        every(lambda k: scattered(k).wait_recv())
        wsum[...] = jnp.sum(wbuf[...].astype(F32), axis=0).astype(BF)
        wall[me] = wsum[...]
        every(lambda k: gather(k).start())

    @pl.when(t >= 2 * steps)
    def _():
        m_ref = m_all.at[u]
        for i in range(0, ib, 2):
            res = nn(rcols[...], m_ref[:, i * out : (i + 2) * out])
            for e in range(2):
                o_ref[i + e] = (res[:, e * out : (e + 1) * out] + b_ref[...]).astype(BF)

    @pl.when(t == 3 * steps - 1)
    def _():
        for k in range(1, ncol):
            left_to(k).wait_send()
            dl_from(k).wait_recv()
            dl_to(k).wait_send()
        got = dlgot[0].astype(F32)
        for k in range(1, ncol):
            got = got + dlgot[k].astype(F32)
        dlown_ref[...] = got.astype(BF)
        to_sib.wait_send()
        for k in range(half):
            forward(k).wait_send()

            @pl.when(jnp.logical_not(is_me(k)))
            def _():
                right_to(k).wait_send()

            @pl.when(owner(k) == me)
            def _():
                keep_part(k).wait()

            @pl.when(owner(k) != me)
            def _():
                to_owner(k).wait_send()
        for k in range(half):
            @pl.when(jnp.logical_not(is_me(k)))
            def _():
                from_row(k).wait_recv()
        summed = part[0].astype(F32)
        for k in range(1, half):
            summed = summed + part[k].astype(F32)
        drown_ref[...] = summed.astype(BF)
        every(lambda k: scatter(k).wait_send())
        every(lambda k: gathered(k).wait_recv())
        every(lambda k: gather(k).wait_send())
        dwall_ref[...] = wall[...]


def apply_layer_norm(x, gain, bias):
    v = x.astype(F32)
    average = jnp.mean(v, axis=-1, keepdims=True)
    shifted = v - average
    variance = jnp.mean(shifted * shifted, axis=-1, keepdims=True)
    inv = lax.rsqrt(variance + 1e-05)
    standard = shifted * inv
    return standard, inv, (standard * gain + bias).astype(BF)


def local(x, gain, bias, wl, bl, wr, br, wo, bo, dp):
    seqs, own, width = x.shape
    hidden = wl.shape[1]
    out = wo.shape[1]
    nrow, ncol = lax.axis_size("row"), lax.axis_size("col")
    sizes = (nrow, ncol)
    total = nrow * ncol
    half = nrow // 2
    rows, cols, _ = dp.shape
    qs = hidden * seqs
    qh = hidden * out
    factor = 1.0 / seqs

    standard, inv, normed = apply_layer_norm(x, gain, bias)
    both = nn(normed.reshape(-1, width), jnp.concatenate([wl, wr], axis=1))
    left = (both[:, :hidden] + bl).astype(BF).reshape(seqs, own, hidden)
    right = (both[:, hidden:] + br).astype(BF).reshape(seqs, own, hidden)
    left_t = left.transpose(2, 1, 0).reshape(hidden, own * seqs)
    right_own = right.transpose(1, 2, 0).reshape(own, qs)

    w2 = wo.reshape(hidden, qh)
    ib = divisor_up_to(rows, 4)
    steps = rows // ib
    dma = pltpu.SemaphoreType.DMA

    def params(n):
        return pltpu.CompilerParams(
            vmem_limit_bytes=56 * 1024 * 1024, collective_id=n, has_side_effects=True
        )

    cost = pl.CostEstimate(flops=8 * cols * qs * rows * out, bytes_accessed=30000000, transcendentals=0)

    def whole(*shape):
        return pl.BlockSpec(shape, lambda t: (0,) * len(shape))

    share = hidden * hidden // total
    update, dw_all, dl_own, dr_own = pl.pallas_call(
        functools.partial(pair_kernel, sizes, ib, seqs, hidden),
        grid=(3 * steps,),
        in_specs=[
            whole(hidden, own * seqs),
            whole(own, qs),
            whole(hidden, qh),
            whole(qh, hidden),
            whole(1, out),
            pl.BlockSpec(
                (ib, cols, out), lambda t: (jnp.where(t < 2 * steps, lax.rem(t, steps), steps - 1), 0, 0)
            ),
        ],
        out_specs=[
            pl.BlockSpec((ib, cols, out), lambda t: (jnp.maximum(t - 2 * steps, 0), 0, 0)),
            whole(total, share, out),
            whole(own * seqs, hidden),
            whole(own, qs),
        ],
        out_shape=[
            jax.ShapeDtypeStruct((rows, cols, out), BF),
            jax.ShapeDtypeStruct((total, share, out), BF),
            jax.ShapeDtypeStruct((own * seqs, hidden), BF),
            jax.ShapeDtypeStruct((own, qs), BF),
        ],
        scratch_shapes=[
            pltpu.VMEM((steps, qs, ib * out), BF),
            pltpu.VMEM((cols, qs), F32),
            pltpu.VMEM((cols, ib * out), BF),
            pltpu.VMEM((ib * seqs, qh), BF),
            pltpu.VMEM((ncol, hidden, own * seqs), BF),
            pltpu.VMEM((hidden, rows * seqs), BF),
            pltpu.VMEM((rows * seqs, hidden), BF),
            pltpu.VMEM((nrow, own, qs), BF),
            pltpu.VMEM((cols, qs), BF),
            pltpu.VMEM((qs, cols), BF),
            pltpu.VMEM((half, 2, own, qs), BF),
            pltpu.VMEM((half, own, qs), BF),
            pltpu.VMEM((half, own, qs), BF),
            pltpu.VMEM((hidden, qh), F32),
            pltpu.VMEM((total, share, out), BF),
            pltpu.VMEM((total, share, out), BF),
            pltpu.VMEM((share, out), BF),
            pltpu.VMEM((total, share, out), BF),
            pltpu.VMEM((rows * seqs, hidden), BF),
            pltpu.VMEM((ncol, own * seqs, hidden), BF),
            dma((ncol,)),
            dma((ncol,)),
            dma((half,)),
            dma((nrow,)),
            dma((half,)),
            dma,
            dma,
            dma((half,)),
            dma((half,)),
            dma((total,)),
            dma((total,)),
            dma((total,)),
            dma((total,)),
            dma((ncol,)),
            dma((ncol,)),
            dma((2,)),
        ],
        compiler_params=params(1),
        cost_estimate=cost,
        name="pair",
    )(left_t, right_own, w2 * BF(factor), w2.T, bo.reshape(1, out), dp)

    dl4 = dl_own.reshape(own, seqs, hidden).transpose(1, 0, 2).reshape(-1, hidden)
    dr4 = dr_own.reshape(own, hidden, seqs).transpose(2, 0, 1).reshape(-1, hidden)
    g = nt(jnp.concatenate([dl4, dr4], axis=1), jnp.concatenate([wl, wr], axis=1))
    g = g.reshape(seqs, own, width) * gain
    centre = jnp.mean(g, axis=-1, keepdims=True)
    slope = jnp.mean(g * standard, axis=-1, keepdims=True)
    dx = (inv * (g - centre - standard * slope)).astype(BF)
    dw_out = dw_all.reshape(hidden, hidden, out).transpose(1, 0, 2).astype(F32)
    return update, dx, dw_out.reshape(hidden * hidden, out)


def solution(mesh):
    both = ("row", "col")
    in_specs = (P(None, both, None),) + (P(),) * 8 + (P("row", "col", None),)
    out_specs = (P("row", "col", None), P(None, both, None), P())
    return jax.shard_map(local, mesh=mesh, in_specs=in_specs, out_specs=out_specs, check_vma=False)
```

time: 282 us -> 112 us (0.40)
  waiting for transfers between devices: 146 us -> 0 us
  blocking collectives: 16.1 us -> 0 us
  between operations: 14.1 us -> 0.86 us
  Pallas kernels: 75.6 us -> 87.2 us
  local copies, waits for them, and re-layouts: 17.2 us -> 13.6 us
    psum x1 -> x0, waiting for transfers between devices: 118 us -> none  [local(): dw_all = lax.psum(dw, ('row', 'col'))]
    reduce_scatter x2 -> x0, waiting for transfers between devices: 24.9 us -> none  [the longest x1 24.9 us: local(): dr_mine = lax.psum_scatter(dr, 'row', scatter_dimension=0, tiled=True)]
    all_gather x1 -> x0, blocking collectives: 16.1 us -> none  [local(): lax.all_gather(left.transpose(1, 0, 2), 'col', axis=0, tiled=True)]
    pallas_call x3 -> x1, Pallas kernels: 75.6 us -> 87.2 us  [local(): pl.pallas_call(functools.partial(pair_kernel, sizes, ib, seqs, hidden), g...]
    all_gather x1 -> x0, waiting for transfers between devices: 3.3 us -> none  [local(): right_cols = lax.all_gather(mine, 'row', axis=0, tiled=True)]
  transfers between devices with their start and end apart: 6 -> 0, of which waited for: 3 -> 0; matrix products, arithmetic and copies ran while one was open for 7% -> 0% of each run, Pallas kernels for 27% -> 0%
where the time goes in v3:
time: 112 us; the launch traced here: 109 us
  Pallas kernels  87.2 us (78%)
  local copies, waits for them, and re-layouts  13.6 us (12%)
  other arithmetic  6.9 us (6%)
    pallas_call x1, Pallas kernels, local(): pl.pallas_call(functools.partial(pair_kernel, sizes, ib, seqs, hidden), g...  87.2 us
    unnamed x20, local copies, waits for them, and re-layouts  3.02 us
    reshape x2, local copies, waits for them, and re-layouts, local(): dl_own.reshape(own, seqs, hidden).transpose(1, 0, 2).reshape(-1, hidden)  2.77 us

profile of v3, /device:TPU:0, one launch (start us, length us, event | category | flops | bytes accessed | tf_op | source)
XLA Modules:
  0.0 109.4 jit_solution(7395126962336885452)
XLA Ops:
  0.6 0.8 constant_dynamic-update-slice_fusion.1
  1.4 0.7 constant_dynamic-update-slice_fusion
  2.1 1.4 %convert_reduce_fusion = f32[64,24]{1,0:T(8,128)S(1)} fusion(bf16[64,24,256]{2,1,0:T(8,128)(2,1)} %param.10), kind=kLoop, calls=%fused_computation.1 | loop fusion | flops 784896 | bytes 792576 | tf_op jit(solution)/shard_map/reduce_sum | solution.py:317
  3.5 0.0 copy-start
  3.6 0.0 copy-start.5
  3.6 0.0 copy-start.6
  3.6 1.7 %fusion.11 = f32[64,24]{1,0:T(8,128)S(1)} fusion(bf16[64,24,256]{2,1,0:T(8,128)(2,1)} %param.10, f32[64,24]{1,0:T(8,128)S(1)} %broadcast_multiply_fusion.2), kind=kLoop, calls=%fused_computation.13 | loop fusion | flops 1571328 | bytes 798720 | tf_op jit(solution)/shard_map/reduce_sum | solution.py:319
  5.3 0.1 reshape.83
  5.4 0.7 broadcast_multiply_fusion.w_ref
  6.2 1.3 %copy.18 = bf16[32,4096]{0,1:T(8,128)(2,1)} copy(bf16[32,4096]{1,0:T(8,128)(2,1)S(1)} %reshape.83) | data formatting | bytes 524288 | tf_op jit(solution)/shard_map/reshape | solution.py:345
  7.5 0.0 copy-done
  7.5 0.5 fusion.6
  8.0 0.4 fusion.19
  8.4 0.1 fusion.12
  8.5 0.8 reshape.81
  9.3 0.8 copy.22.r_ref
  10.1 0.8 reshape.79
  10.9 0.2 copy.16
  11.2 0.8 reshape.80.lt_ref
  12.0 87.2 %pair.1 = (bf16[48,384,128]{2,1,0:T(8,128)(2,1)}, bf16[32,32,128]{2,1,0:T(8,128)(2,1)}, bf16[1536,32]{1,0:T(8,128)(2,1)}, bf16[24,2048]{1,0:T(8,128)(2,1)}) custom-call(bf16[32,1536]{1,0:T(8,128)(2,1)} %reshape.80.lt_ref, bf16[24,2048]{1,0:T(8,128)(2,1)} %copy.22.r_ref, bf16[32,4096]{1,0:T(8,128)(2,1)} %broadcast_multiply_fusion.w_ref, ...), custom_call_target="tpu_custom_call" | custom-call | flops 38654705664 | bytes 30000000 | tf_op jit(solution)/shard_map/pair/pallas_call | solution.py:361
  99.2 2.1 %copy.19 = bf16[24,64,32]{0,1,2:T(8,128)(2,1)S(1)} copy(bf16[24,64,32]{2,1,0:T(8,128)(2,1)} %bitcast.36) | data formatting | bytes 196608 | tf_op jit(solution)/shard_map/reshape | solution.py:429
  101.2 0.7 reshape.86
  102.0 0.3 copy.23
  102.2 0.7 reshape.88
  102.9 0.1 convert_bitcast_fusion
  103.0 1.1 %copy.21 = f32[32,32,128]{2,1,0:T(8,128)} copy(f32[32,32,128]{2,0,1:T(8,128)S(1)} %convert_bitcast_fusion) | data formatting | bytes 1048576 | tf_op jit(solution)/shard_map/reshape | solution.py:437
  104.1 0.5 multiply_reduce_fusion
  104.6 0.1 div.17
  104.7 0.7 fusion.7
  105.4 1.7 %fusion.10 = bf16[64,24,256]{2,1,0:T(8,128)(2,1)} fusion(bf16[64,24,256]{2,1,0:T(8,128)(2,1)S(1)} %copy-done, f32[64,24,256]{2,1,0:T(8,128)S(1)} %bitcast.28, f32[64,24]{1,0:T(8,128)S(1)} %broadcast_multiply_fusion.1, f32[64,24]{1,0:T(8,128)S(1)} %div.17, f32[256]{0:T(256)S(1)} %copy-done.5, f32[64,24]{1,0:T(8,128)S(1)} %add_rsqrt_fusion, ...), kind=kLoop, calls=%fused_computation.12 | loop fusion | flops 3538944 | bytes 3171328 | tf_op jit(solution)/shard_map/convert_element_type | solution.py:435
  107.2 0.0 copy-done.1
  107.2 2.2 %copy.26 = bf16[48,384,128]{2,1,0:T(8,128)(2,1)} copy(bf16[48,384,128]{2,1,0:T(8,128)(2,1)S(1)} %copy-done.1) | data formatting | bytes 9437184
  (17 shorter events, 0.1 us)
Async XLA Ops:
  0.6 4.7 %copy-start.3 = (bf16[1024,128]{1,0:T(8,128)(2,1)S(1)}, bf16[1024,128]{1,0:T(8,128)(2,1)}, u32[]{:S(2)}) copy-start(bf16[1024,128]{1,0:T(8,128)(2,1)} %param.17) | copy-start | bytes 786436
  3.5 3.9 %copy-start = (bf16[64,24,256]{2,1,0:T(8,128)(2,1)S(1)}, bf16[64,24,256]{2,1,0:T(8,128)(2,1)}, u32[]{:S(2)}) copy-start(bf16[64,24,256]{2,1,0:T(8,128)(2,1)} %param.10) | copy-start | bytes 2359300
  3.6 3.9 %copy-start.5 = (f32[256]{0:T(256)S(1)}, f32[256]{0:T(256)}, u32[]{:S(2)}) copy-start(f32[256]{0:T(256)} %param.11) | copy-start | bytes 3076
  3.6 3.9 %copy-start.6 = (f32[256]{0:T(256)S(1)}, f32[256]{0:T(256)}, u32[]{:S(2)}) copy-start(f32[256]{0:T(256)} %param.12) | copy-start | bytes 3076
  7.5 0.9 copy-start.7
  7.5 0.9 copy-start.8
  99.2 2.8 %copy-start.4 = (bf16[24,2048]{1,0:T(8,128)(2,1)S(1)}, bf16[24,2048]{1,0:T(8,128)(2,1)}, u32[]{:S(2)}) copy-start(bf16[24,2048]{1,0:T(8,128)(2,1)} %get-tuple-element.9) | copy-start | bytes 294916
  99.2 3.8 %copy-start.2 = (bf16[32,32,128]{2,1,0:T(8,128)(2,1)S(1)}, bf16[32,32,128]{2,1,0:T(8,128)(2,1)}, u32[]{:S(2)}) copy-start(bf16[32,32,128]{2,1,0:T(8,128)(2,1)} %get-tuple-element.10) | copy-start | bytes 786436
  104.7 2.5 %copy-start.1 = (bf16[48,384,128]{2,1,0:T(8,128)(2,1)S(1)}, bf16[48,384,128]{2,1,0:T(8,128)(2,1)}, u32[]{:S(2)}) copy-start(bf16[48,384,128]{2,1,0:T(8,128)(2,1)} %get-tuple-element.18) | copy-start | bytes 14155780
